TPU v7x, 512 devices: a whole 4x4x16 slice. The times are simulated.
512 devices in a mesh: wide: 128 (over z, y, core), narrow: 4 (over x).
Axes of the slice: x: 4, y: 4, z: 16, core: 2. Of those that a mesh axis runs over, the one named last changes fastest.
Arguments:
- coefficients: bfloat16 [100, 2097152], P(None, ('wide', 'narrow')), may hold values from -6 to 6
- neighbours: int32 [4, 2097152], P(None, ('wide', 'narrow')), may hold values from 0 to 5119
- halo_blocks: int32 [512, 4, 2], P(('wide', 'narrow')), may hold values from 0 to 31, as said below
- recon_weight: bfloat16 [5, 75, 100], replicated, may hold values from -0.25 to 0.25
- owner_device: int32 [16384], P(('wide', 'narrow')), may hold values from 0 to 511, as said below
- work_count: int32 [16384], P(('wide', 'narrow')), may hold values from 1 to 4
Outputs:
- migrated_modal: bfloat16 [100, 2097152], P(None, ('wide', 'narrow'))
- migrated_metric: float32 [6, 2097152], P(None, ('wide', 'narrow'))
- migrated_work: float32 [2097152], P(('wide', 'narrow'))
Inputs may be any that keep to these rules, and one draw needn't show every extreme that they name: `halo_blocks`: each device's list for one direction holds 2 different block numbers of that device. `owner_device`: every device receives exactly 32 blocks. Of one device's blocks, either exactly 1 or none go to devices of any one wide index. Two devices of the same wide index with narrow indices 2j and 2j + 1 together send either exactly 1 or none of their blocks to devices of any one wide index. For every wide index w and narrow indices a and c, exactly 8 of the blocks that devices of narrow index a send to wide index w go to the device of wide index w and narrow index c.
All inputs are finite; a program needn't handle non-finite values.
Results may differ from a plain program's by a relative error of at most 0.0004.
Values may be sent and summed in bfloat16 or wider, within the bound.
A program may use at most 64 MiB of HBM per device.

v0:
```python
import jax
import jax.numpy as jnp
from jax import lax
from jax.sharding import PartitionSpec as P


def passed_along(value, axis, steps):
    count = lax.axis_size(axis)
    pairs = [(source, (source + steps) % count) for source in range(count)]
    return lax.ppermute(value, axis, pairs)


def swapped(value, axis, apart):
    return lax.ppermute(value, axis, [(i, i ^ 1 << apart) for i in range(lax.axis_size(axis))])


def metric_rows(derivs):
    vectors = derivs.reshape(derivs.shape[0] // 3, 3, derivs.shape[1])
    inverse = 1.0 / vectors.shape[0]
    along_x = vectors[:, 0]
    along_y = vectors[:, 1]
    along_z = vectors[:, 2]
    return jnp.stack(
        [
            1.0 + inverse * jnp.sum(along_x * along_x, axis=0),
            1.0 + inverse * jnp.sum(along_y * along_y, axis=0),
            1.0 + inverse * jnp.sum(along_z * along_z, axis=0),
            inverse * jnp.sum(along_x * along_y, axis=0),
            inverse * jnp.sum(along_x * along_z, axis=0),
            inverse * jnp.sum(along_y * along_z, axis=0),
        ]
    )


def determinant(components):
    metric_xx = components[0]
    metric_yy = components[1]
    metric_zz = components[2]
    metric_xy = components[3]
    metric_xz = components[4]
    metric_yz = components[5]
    return (
        metric_xx * (metric_yy * metric_zz - metric_yz * metric_yz)
        - metric_xy * (metric_xy * metric_zz - metric_yz * metric_xz)
        + metric_xz * (metric_xy * metric_yz - metric_yy * metric_xz)
    )


def first_slots(slot_of, slot_total, position):
    slot_ids = jnp.arange(slot_total, dtype=jnp.int32)
    matches = slot_of[None, :] == slot_ids[:, None]
    filled = jnp.any(matches, axis=1)
    picked = jnp.sum(jnp.where(matches, position[None, :], 0), axis=1)
    return (filled, picked)


def per_device(coefficients, neighbours, halo_blocks, recon_weight, owner_device, work_count):
    coeff_count, elem_count = coefficients.shape
    block_count = owner_device.shape[0]
    block_len = elem_count // block_count
    halo_count = halo_blocks.shape[2]
    wide_size = lax.axis_size("wide")
    narrow_size = lax.axis_size("narrow")
    blocked = coefficients.reshape(coeff_count, block_count, block_len)
    sending = halo_blocks[0]

    def outgoing(direction):
        return jnp.take(blocked, sending[direction], axis=1)

    def from_wide(block_set, offset):
        return passed_along(block_set, "wide", offset)

    def from_narrow(block_set, offset):
        return passed_along(block_set, "narrow", offset)

    arrived = [
        from_wide(outgoing(1), 1),
        from_wide(outgoing(0), -1),
        from_narrow(outgoing(3), 1),
        from_narrow(outgoing(2), -1),
    ]
    halo_cols = jnp.concatenate(arrived, axis=1).reshape(coeff_count, 4 * halo_count * block_len)
    derivs = jnp.dot(recon_weight[0], coefficients, preferred_element_type=jnp.float32)
    extended = jnp.concatenate([coefficients, halo_cols], axis=1)
    for face_index in range(4):
        gathered = jnp.take(extended, neighbours[face_index], axis=1)
        derivs = derivs + jnp.dot(
            recon_weight[face_index + 1], gathered, preferred_element_type=jnp.float32
        )
    components = metric_rows(derivs)
    work_est = jnp.repeat(work_count.astype(jnp.float32), block_len) * jnp.sqrt(
        determinant(components)
    )
    components, work_est = lax.optimization_barrier((components, work_est))
    stats = jnp.concatenate([components, work_est[None, :]], axis=0).reshape(
        7, block_count, block_len
    )
    wide_target = owner_device // narrow_size
    narrow_target = owner_device % narrow_size
    position = jnp.arange(block_count, dtype=jnp.int32)
    earlier = (wide_target[None, :] == wide_target[:, None]) & (
        position[None, :] < position[:, None]
    )
    rank_of = jnp.sum(earlier.astype(jnp.int32), axis=1)
    member = lax.axis_index("narrow") % 2
    other = 1 - member
    half_len = block_len // 2
    pair_wide = max(1, 2 * block_count // wide_size)
    pair_total = wide_size * pair_wide
    pair_ids = jnp.arange(pair_total, dtype=jnp.int32)
    pair_slot = wide_target * pair_wide + rank_of
    own_coeffs = lax.dynamic_slice_in_dim(blocked, member * half_len, half_len, 2)
    own_stats = lax.dynamic_slice_in_dim(stats, member * half_len, half_len, 2)
    give_coeffs = lax.dynamic_slice_in_dim(blocked, other * half_len, half_len, 2)
    give_stats = lax.dynamic_slice_in_dim(stats, other * half_len, half_len, 2)
    labels = jnp.stack([pair_slot, narrow_target]).astype(jnp.float32)
    partner_coeffs = swapped(give_coeffs, "narrow", 0)
    partner_stats, partner_labels = swapped((give_stats, labels), "narrow", 0)
    partner_slot = partner_labels[0].astype(jnp.int32)
    partner_target = partner_labels[1].astype(jnp.int32)
    own_has, own_pick = first_slots(pair_slot, pair_total, position)
    partner_has, partner_pick = first_slots(partner_slot, pair_total, position)
    zero_coeff = jnp.zeros((), blocked.dtype)
    joined_coeffs = jnp.where(
        own_has[None, :, None],
        jnp.take(own_coeffs, own_pick, axis=1),
        jnp.where(
            partner_has[None, :, None], jnp.take(partner_coeffs, partner_pick, axis=1), zero_coeff
        ),
    )
    joined_stats = jnp.where(
        own_has[None, :, None],
        jnp.take(own_stats, own_pick, axis=1),
        jnp.where(partner_has[None, :, None], jnp.take(partner_stats, partner_pick, axis=1), 0.0),
    )
    pair_tags = jnp.where(
        own_has,
        jnp.take(narrow_target, own_pick) * 2 + member,
        jnp.where(partner_has, jnp.take(partner_target, partner_pick) * 2 + other, -1),
    )
    stats_in, tags_in = (
        lax.all_to_all(joined_stats, "wide", split_axis=1, concat_axis=1, tiled=True),
        lax.all_to_all(
            pair_tags.astype(jnp.float32)[None, :], "wide", split_axis=1, concat_axis=1, tiled=True
        ),
    )
    coeffs_in = lax.all_to_all(joined_coeffs, "wide", split_axis=1, concat_axis=1, tiled=True)
    arrived_tags = tags_in[0].astype(jnp.int32)
    anchor = jnp.where(arrived_tags >= 0, arrived_tags % 2, -1)
    keep_order = jnp.argsort(jnp.where(anchor == member, 0, 1) * pair_total + pair_ids)[
        :block_count
    ]
    pass_order = jnp.argsort(jnp.where(anchor == other, 0, 1) * pair_total + pair_ids)[:block_count]
    returned_coeffs = swapped(jnp.take(coeffs_in, pass_order, axis=1), "narrow", 0)
    returned_stats = swapped(jnp.take(stats_in, pass_order, axis=1), "narrow", 0)
    kept_coeffs = jnp.take(coeffs_in, keep_order, axis=1)
    kept_stats = jnp.take(stats_in, keep_order, axis=1)
    at_front = member == 0
    whole_coeffs = jnp.concatenate(
        [
            jnp.where(at_front, kept_coeffs, returned_coeffs),
            jnp.where(at_front, returned_coeffs, kept_coeffs),
        ],
        axis=2,
    )
    whole_stats = jnp.concatenate(
        [
            jnp.where(at_front, kept_stats, returned_stats),
            jnp.where(at_front, returned_stats, kept_stats),
        ],
        axis=2,
    )
    through = jnp.argsort(jnp.take(arrived_tags, keep_order) // 2 * block_count + position)
    relayed_coeffs = jnp.take(whole_coeffs, through, axis=1)
    relayed_stats = jnp.take(whole_stats, through, axis=1)
    new_coeffs = lax.all_to_all(relayed_coeffs, "narrow", split_axis=1, concat_axis=1, tiled=True)
    new_stats = lax.all_to_all(relayed_stats, "narrow", split_axis=1, concat_axis=1, tiled=True)
    flat_stats = new_stats.reshape(7, elem_count)
    return (new_coeffs.reshape(coeff_count, elem_count), flat_stats[:6], flat_stats[6])


def solution(mesh):
    return jax.shard_map(
        per_device,
        mesh=mesh,
        in_specs=(
            P(None, ("wide", "narrow")),
            P(None, ("wide", "narrow")),
            P(("wide", "narrow"), None, None),
            P(),
            P(("wide", "narrow")),
            P(("wide", "narrow")),
        ),
        out_specs=(P(None, ("wide", "narrow")), P(None, ("wide", "narrow")), P(("wide", "narrow"))),
        check_vma=False,
    )
```

profile of v0, /device:TPU:32, one launch (start us, length us, event | category | flops | bytes accessed | tf_op | source)
XLA Modules:
  0.0 322.5 jit_solution(11149431525572227855)
XLA Ops:
  0.6 1.0 slice_reduce_fusion.3
  1.7 1.6 copy.50
  3.4 0.7 copy.53
  4.0 0.6 gather_fusion.9
  4.7 2.0 collective-permute-start.3
  7.4 5.7 %collective-permute-start.4 = (bf16[100,2,128]{2,0,1:T(8,128)(2,1)S(1)}, bf16[100,2,128]{2,0,1:T(8,128)(2,1)S(1)}, u32[]{:S(2)}, u32[]{:S(2)}) collective-permute-start(bf16[100,2,128]{2,0,1:T(8,128)(2,1)S(1)} %select_bitcast_fusion.6), channel_id=1, source_target_pairs={{0,508},{4,0},{8,4},{12,8},{16,12},{20,16},{24,20},{28,24},{32,28}... | collective-permute-start | bytes 153608 | tf_op jit(solution)/shard_map/ppermute | solution.py:10
  13.9 3.4 %collective-permute-start.5 = (bf16[100,2,128]{2,0,1:T(8,128)(2,1)S(1)}, bf16[100,2,128]{2,0,1:T(8,128)(2,1)S(1)}, u32[]{:S(2)}, u32[]{:S(2)}) collective-permute-start(bf16[100,2,128]{2,0,1:T(8,128)(2,1)S(1)} %select_bitcast_fusion.5), channel_id=1, source_target_pairs={{0,1},{1,2},{2,3},{3,0},{4,5},{5,6},{6,7},{7,4},{8,9},{9,10},{10,1... | collective-permute-start | bytes 153608 | tf_op jit(solution)/shard_map/ppermute | solution.py:10
  17.9 3.6 %collective-permute-start.6 = (bf16[100,2,128]{2,0,1:T(8,128)(2,1)S(1)}, bf16[100,2,128]{2,0,1:T(8,128)(2,1)S(1)}, u32[]{:S(2)}, u32[]{:S(2)}) collective-permute-start(bf16[100,2,128]{2,0,1:T(8,128)(2,1)S(1)} %select_bitcast_fusion.4), channel_id=1, source_target_pairs={{0,3},{1,0},{2,1},{3,2},{4,7},{5,4},{6,5},{7,6},{8,11},{9,8},{10,9... | collective-permute-start | bytes 153608 | tf_op jit(solution)/shard_map/ppermute | solution.py:10
  21.8 2.2 collective-permute-start
  24.9 1.4 fusion.28
  26.4 0.6 convert_element_type.36
  27.0 1.2 gather_fusion.3
  28.5 1.2 gather_fusion.4
  30.8 14.9 %gather_fusion.13 = bf16[4096,100]{1,0:T(8,128)(2,1)} fusion(bf16[100,5120]{0,1:T(8,128)(2,1)S(1)} %pad_maximum_fusion, s32[4096]{0:T(1024)S(1)} %fusion.38), kind=kCustom, calls=%fused_computation.4.clone | custom fusion | bytes 1654784 | tf_op jit(solution)/shard_map/jit(_take)/gather | solution.py:86
  45.7 14.9 %gather_fusion.14 = bf16[4096,100]{1,0:T(8,128)(2,1)} fusion(bf16[100,5120]{0,1:T(8,128)(2,1)S(1)} %pad_maximum_fusion, s32[4096]{0:T(1024)S(1)} %fusion.39), kind=kCustom, calls=%fused_computation.13.clone | custom fusion | bytes 1654784 | tf_op jit(solution)/shard_map/jit(_take)/gather | solution.py:86
  60.6 14.9 %gather_fusion.15 = bf16[4096,100]{1,0:T(8,128)(2,1)} fusion(bf16[100,5120]{0,1:T(8,128)(2,1)S(1)} %pad_maximum_fusion, s32[4096]{0:T(1024)S(1)} %fusion.40), kind=kCustom, calls=%fused_computation.14.clone | custom fusion | bytes 1654784 | tf_op jit(solution)/shard_map/jit(_take)/gather | solution.py:86
  75.4 12.1 %gather_fusion.16 = bf16[4096,100]{1,0:T(8,128)(2,1)S(1)} fusion(bf16[100,5120]{0,1:T(8,128)(2,1)S(1)} %pad_maximum_fusion, s32[4096]{0:T(1024)S(1)} %fusion.41), kind=kCustom, calls=%fused_computation.15.clone | custom fusion | bytes 1654784 | tf_op jit(solution)/shard_map/jit(_take)/gather | solution.py:86
  87.6 2.5 fusion.3
  90.1 0.8 fusion.2
  91.4 0.8 fusion.1
  92.2 0.8 fusion
  93.0 1.7 reshape.171
  94.8 4.4 %multiply_reduce_fusion = (f32[4096]{0:T(1024)S(1)}, f32[4096]{0:T(1024)S(1)}, f32[4096]{0:T(1024)S(1)}, f32[4096]{0:T(1024)S(1)}, f32[4096]{0:T(1024)S(1)}, /*index=5*/f32[4096]{0:T(1024)S(1)}) fusion(f32[25,3,4096]{2,1,0:T(4,128)} %reshape.171), kind=kLoop, calls=%fused_computation.56 | loop fusion | flops 1204224 | bytes 1327104 | tf_op jit(solution)/shard_map/reduce_sum | solution.py:30
  99.6 3.6 %collective-permute-start.7 = (f32[7,32,64]{2,0,1:T(8,128)S(1)}, f32[7,32,64]{2,0,1:T(8,128)S(1)}, u32[]{:S(2)}, u32[]{:S(2)}) collective-permute-start(f32[7,32,64]{2,0,1:T(8,128)S(1)} %get-tuple-element.43), channel_id=1, source_target_pairs={{0,1},{1,0},{2,3},{3,2},{4,5},{5,4},{6,7},{7,6},{8,9},{9,8},{10,11... | collective-permute-start | bytes 172040 | tf_op jit(solution)/shard_map/ppermute | solution.py:14
  103.3 0.7 copy.49
  104.0 17.8 %all-to-all-start = ((f32[1,128,1]{2,0,1:T(1,128)}), f32[1,128,1]{2,0,1:T(1,128)S(1)}, u32[]{:S(2)}, u32[]{:S(2)}) async-start(f32[1,128,1]{2,0,1:T(1,128)} %copy.49), calls=%async_computation | async-start | bytes 131072 | tf_op jit(solution)/shard_map/all_to_all | solution.py:143
  121.8 0.8 gather_fusion.17
  122.6 0.8 gather_fusion.18
  123.4 0.8 fusion.56
  124.2 1.1 reshape.403
  125.3 10.8 %all-to-all-done = f32[1,128,1]{2,0,1:T(1,128)S(1)} async-done(((f32[1,128,1]{2,0,1:T(1,128)}), f32[1,128,1]{2,0,1:T(1,128)S(1)}, u32[]{:S(2)}, u32[]{:S(2)}) %all-to-all-start) | async-done | bytes 544 | tf_op jit(solution)/shard_map/all_to_all | solution.py:143
  136.1 6.2 %all-to-all-start.3 = ((f32[128,1,448]{2,1,0:T(1,128)}), f32[128,1,448]{2,1,0:T(1,128)S(1)}, u32[]{:S(2)}, u32[]{:S(2)}) async-start(f32[128,1,448]{2,1,0:T(1,128)} %reshape.403), calls=%async_computation.3 | async-start | bytes 524288 | tf_op jit(solution)/shard_map/all_to_all | solution.py:142
  142.4 0.9 constant_dynamic-slice_fusion.1
  143.2 2.2 collective-permute-start.1
  145.4 1.0 gather_fusion.5
  146.4 12.9 %collective-permute-done.1 = bf16[100,32,64]{0,2,1:T(8,128)(2,1)S(1)} collective-permute-done((bf16[100,32,64]{0,2,1:T(8,128)(2,1)}, bf16[100,32,64]{0,2,1:T(8,128)(2,1)S(1)}, u32[]{:S(2)}, u32[]{:S(2)}) %collective-permute-start.1) | collective-permute-done | bytes 409632 | tf_op jit(solution)/shard_map/ppermute | solution.py:14
  159.3 2.2 gather_fusion.6
  161.5 3.3 %fusion.4 = bf16[100,128,64]{0,2,1:T(8,128)(2,1)} fusion(bf16[128,100,64]{1,2,0:T(8,128)(2,1)} %gather_fusion.6, bf16[128,100,64]{1,2,0:T(8,128)(2,1)S(1)} %gather_fusion.5, pred[128]{0:T(512)(128)(4,1)S(1)} %compare_and_fusion.9, pred[128]{0:T(512)(128)(4,1)S(1)} %copy-done.7, pred[128]{0:T(512)(128)(4,1)S(1)} %copy-done.6, pred[128]{0:T(512)(128)(4,1)S(1)} %fusion.36), kind=kLoop, calls=%fused_computation.30 | loop fusion | flops 3276800 | bytes 4915712 | tf_op jit(solution)/shard_map/jit(_where)/select_n | solution.py:124
  164.9 16.0 %all-to-all-start.1 = ((bf16[100,128,64]{0,2,1:T(8,128)(2,1)}), bf16[100,128,64]{0,2,1:T(8,128)(2,1)S(1)}, u32[]{:S(2)}, u32[]{:S(2)}) async-start(bf16[100,128,64]{0,2,1:T(8,128)(2,1)} %fusion.4), calls=%async_computation.1 | async-start | bytes 4194304 | tf_op jit(solution)/shard_map/all_to_all | solution.py:147
  180.9 2.4 convert_reduce_fusion
  183.3 2.5 sort.48
  185.9 0.7 gather_fusion
  186.6 2.5 sort.50
  189.1 1.6 sort.49
  191.3 1.3 reduce.16
  192.7 0.6 gather_fusion.20
  193.4 2.2 collective-permute-start.8
  195.6 0.6 gather_fusion.19
  196.2 4.6 %collective-permute-done.8 = f32[7,32,64]{2,0,1:T(8,128)S(1)} collective-permute-done((f32[7,32,64]{2,0,1:T(8,128)S(1)}, f32[7,32,64]{2,0,1:T(8,128)S(1)}, u32[]{:S(2)}, u32[]{:S(2)}) %collective-permute-start.8) | collective-permute-done | bytes 57376 | tf_op jit(solution)/shard_map/ppermute | solution.py:14
  201.0 78.2 %all-to-all-done.1 = bf16[100,128,64]{0,2,1:T(8,128)(2,1)S(1)} async-done(((bf16[100,128,64]{0,2,1:T(8,128)(2,1)}), bf16[100,128,64]{0,2,1:T(8,128)(2,1)S(1)}, u32[]{:S(2)}, u32[]{:S(2)}) %all-to-all-start.1) | async-done | bytes 1638432 | tf_op jit(solution)/shard_map/all_to_all | solution.py:147
  279.1 0.6 gather_fusion.8
  279.9 2.2 collective-permute-start.2
  282.2 0.6 gather_fusion.2
  282.9 15.9 %all_to_all.29 = f32[7,32,128]{2,0,1:T(8,128)S(1)} all-to-all(f32[7,32,128]{2,0,1:T(8,128)S(1)} %select_bitcast_fusion.3), channel_id=1, replica_groups=mesh['wide'=128,'narrow'=4] {'narrow'}, dimensions={1} | all-to-all | bytes 229376 | tf_op jit(solution)/shard_map/all_to_all | solution.py:177
  298.9 0.6 slice.143
  299.5 0.6 gather_fusion.7
  300.2 1.2 bitcast_select_fusion.3
  301.6 0.7 copy.51
  302.3 0.7 gather_fusion.1
  303.0 1.0 select_bitcast_fusion
  304.1 3.5 %all-to-all-start.2 = ((bf16[100,32,128]{2,0,1:T(8,128)(2,1)}), bf16[100,32,128]{2,0,1:T(8,128)(2,1)S(1)}, u32[]{:S(2)}, u32[]{:S(2)}) async-start(bf16[100,32,128]{2,0,1:T(8,128)(2,1)} %select_bitcast_fusion), calls=%async_computation.2 | async-start | bytes 1703936 | tf_op jit(solution)/shard_map/all_to_all | solution.py:176
  307.6 0.7 slice_bitcast_fusion
  308.2 12.8 %all-to-all-done.2 = bf16[100,32,128]{2,0,1:T(8,128)(2,1)S(1)} async-done(((bf16[100,32,128]{2,0,1:T(8,128)(2,1)}), bf16[100,32,128]{2,0,1:T(8,128)(2,1)S(1)}, u32[]{:S(2)}, u32[]{:S(2)}) %all-to-all-start.2) | async-done | bytes 819232 | tf_op jit(solution)/shard_map/all_to_all | solution.py:176
  321.3 1.2 copy.62
  (109 shorter events, 7.1 us)
Async XLA Ops:
  3.3 18.3 %copy-start.12 = (s32[32]{0:T(128)S(1)}, s32[32]{0:T(128)}, u32[]{:S(2)}) copy-start(s32[32]{0:T(128)} %param.24) | copy-start | bytes 388
  3.3 20.7 %copy-start.4 = (s32[4,4096]{1,0:T(4,128)S(1)}, s32[4,4096]{1,0:T(4,128)}, u32[]{:S(2)}) copy-start(s32[4,4096]{1,0:T(4,128)} %param.21) | copy-start | bytes 196612
  3.3 21.6 %copy-start.2 = (bf16[100,4096]{1,0:T(8,128)(2,1)S(1)}, bf16[100,4096]{1,0:T(8,128)(2,1)}, u32[]{:S(2)}) copy-start(bf16[100,4096]{1,0:T(8,128)(2,1)} %param.20) | copy-start | bytes 2457604
  3.3 21.6 %copy-start.3 = (bf16[5,75,100]{2,1,0:T(8,128)(2,1)S(1)}, bf16[5,75,100]{2,1,0:T(8,128)(2,1)}, u32[]{:S(2)}) copy-start(bf16[5,75,100]{2,1,0:T(8,128)(2,1)} %param.23) | copy-start | bytes 225004
  4.7 21.7 %copy-start.13 = (s32[32]{0:T(128)S(1)}, s32[32]{0:T(128)}, u32[]{:S(2)}) copy-start(s32[32]{0:T(128)} %param.25) | copy-start | bytes 388
  4.7 25.6 %collective-permute-start.3 = (bf16[100,2,128]{2,0,1:T(8,128)(2,1)S(1)}, bf16[100,2,128]{2,0,1:T(8,128)(2,1)S(1)}, u32[]{:S(2)}, u32[]{:S(2)}) collective-permute-start(bf16[100,2,128]{2,0,1:T(8,128)(2,1)S(1)} %select_bitcast_fusion.7), channel_id=1, source_target_pairs={{0,4},{4,8},{8,12},{12,16},{16,20},{20,24},{24,28},{28,32},{32,36}... | collective-permute-start | bytes 153608 | tf_op jit(solution)/shard_map/ppermute | solution.py:10
  7.4 22.8 %collective-permute-start.4 = (bf16[100,2,128]{2,0,1:T(8,128)(2,1)S(1)}, bf16[100,2,128]{2,0,1:T(8,128)(2,1)S(1)}, u32[]{:S(2)}, u32[]{:S(2)}) collective-permute-start(bf16[100,2,128]{2,0,1:T(8,128)(2,1)S(1)} %select_bitcast_fusion.6), channel_id=1, source_target_pairs={{0,508},{4,0},{8,4},{12,8},{16,12},{20,16},{24,20},{28,24},{32,28}... | collective-permute-start | bytes 153608 | tf_op jit(solution)/shard_map/ppermute | solution.py:10
  13.9 16.4 %collective-permute-start.5 = (bf16[100,2,128]{2,0,1:T(8,128)(2,1)S(1)}, bf16[100,2,128]{2,0,1:T(8,128)(2,1)S(1)}, u32[]{:S(2)}, u32[]{:S(2)}) collective-permute-start(bf16[100,2,128]{2,0,1:T(8,128)(2,1)S(1)} %select_bitcast_fusion.5), channel_id=1, source_target_pairs={{0,1},{1,2},{2,3},{3,0},{4,5},{5,6},{6,7},{7,4},{8,9},{9,10},{10,1... | collective-permute-start | bytes 153608 | tf_op jit(solution)/shard_map/ppermute | solution.py:10
  17.9 12.3 %collective-permute-start.6 = (bf16[100,2,128]{2,0,1:T(8,128)(2,1)S(1)}, bf16[100,2,128]{2,0,1:T(8,128)(2,1)S(1)}, u32[]{:S(2)}, u32[]{:S(2)}) collective-permute-start(bf16[100,2,128]{2,0,1:T(8,128)(2,1)S(1)} %select_bitcast_fusion.4), channel_id=1, source_target_pairs={{0,3},{1,0},{2,1},{3,2},{4,7},{5,4},{6,5},{7,6},{8,11},{9,8},{10,9... | collective-permute-start | bytes 153608 | tf_op jit(solution)/shard_map/ppermute | solution.py:10
  21.8 6.4 %collective-permute-start = (f32[2,32]{1,0:T(2,128)S(1)}, f32[2,32]{1,0:T(2,128)S(1)}, u32[]{:S(2)}, u32[]{:S(2)}) collective-permute-start(f32[2,32]{1,0:T(2,128)S(1)} %add_convert_fusion), channel_id=1, source_target_pairs={{0,1},{1,0},{2,3},{3,2},{4,5},{5,4},{6,7},{7,6},{8,9},{9,8},{10,11... | collective-permute-start | bytes 776 | tf_op jit(solution)/shard_map/ppermute | solution.py:14
  28.4 2.4 copy-start.10
  28.4 2.3 copy-start.5
  87.6 2.6 copy-start.1
  90.1 1.2 copy-start
  93.0 6.1 %copy-start.9 = (f32[32]{0:T(128)S(1)}, f32[32]{0:T(128)}, u32[]{:S(2)}) copy-start(f32[32]{0:T(128)} %convert_element_type.36) | copy-start | bytes 388
  94.7 8.5 %copy-start.11 = (s32[128]{0:T(128)S(1)}, s32[128]{0:T(128)}, u32[]{:S(2)}) copy-start(s32[128]{0:T(128)} %copy-done.10) | copy-start | bytes 1540
  94.8 8.5 %copy-start.8 = (f32[1,128,1]{1,2,0:T(1,128)S(1)}, f32[1,128,1]{1,2,0:T(1,128)}, u32[]{:S(2)}) copy-start(f32[1,128,1]{1,2,0:T(1,128)} %convert_bitcast_fusion) | copy-start | bytes 1540
  99.1 24.2 %copy-start.6 = (pred[128]{0:T(512)(128)(4,1)S(1)}, pred[128]{0:T(512)(128)(4,1)}, u32[]{:S(2)}) copy-start(pred[128]{0:T(512)(128)(4,1)} %copy-done.5) | copy-start | bytes 388
  99.1 24.2 %copy-start.7 = (pred[128]{0:T(512)(128)(4,1)S(1)}, pred[128]{0:T(512)(128)(4,1)}, u32[]{:S(2)}) copy-start(pred[128]{0:T(512)(128)(4,1)} %compare_and_fusion.10) | copy-start | bytes 388
  99.6 23.0 %collective-permute-start.7 = (f32[7,32,64]{2,0,1:T(8,128)S(1)}, f32[7,32,64]{2,0,1:T(8,128)S(1)}, u32[]{:S(2)}, u32[]{:S(2)}) collective-permute-start(f32[7,32,64]{2,0,1:T(8,128)S(1)} %get-tuple-element.43), channel_id=1, source_target_pairs={{0,1},{1,0},{2,3},{3,2},{4,5},{5,4},{6,7},{7,6},{8,9},{9,8},{10,11... | collective-permute-start | bytes 172040 | tf_op jit(solution)/shard_map/ppermute | solution.py:14
  104.0 32.1 %all-to-all-start = ((f32[1,128,1]{2,0,1:T(1,128)}), f32[1,128,1]{2,0,1:T(1,128)S(1)}, u32[]{:S(2)}, u32[]{:S(2)}) async-start(f32[1,128,1]{2,0,1:T(1,128)} %copy.49), calls=%async_computation | async-start | bytes 131072 | tf_op jit(solution)/shard_map/all_to_all | solution.py:143
  136.1 28.8 %all-to-all-start.3 = ((f32[128,1,448]{2,1,0:T(1,128)}), f32[128,1,448]{2,1,0:T(1,128)S(1)}, u32[]{:S(2)}, u32[]{:S(2)}) async-start(f32[128,1,448]{2,1,0:T(1,128)} %reshape.403), calls=%async_computation.3 | async-start | bytes 524288 | tf_op jit(solution)/shard_map/all_to_all | solution.py:142
  143.2 16.1 %collective-permute-start.1 = (bf16[100,32,64]{0,2,1:T(8,128)(2,1)}, bf16[100,32,64]{0,2,1:T(8,128)(2,1)S(1)}, u32[]{:S(2)}, u32[]{:S(2)}) collective-permute-start(bf16[100,32,64]{0,2,1:T(8,128)(2,1)} %get-tuple-element.39), channel_id=1, source_target_pairs={{0,1},{1,0},{2,3},{3,2},{4,5},{5,4},{6,7},{7,6},{8,9},{9,8},{10,11... | collective-permute-start | bytes 1228808 | tf_op jit(solution)/shard_map/ppermute | solution.py:14
  164.9 114.2 %all-to-all-start.1 = ((bf16[100,128,64]{0,2,1:T(8,128)(2,1)}), bf16[100,128,64]{0,2,1:T(8,128)(2,1)S(1)}, u32[]{:S(2)}, u32[]{:S(2)}) async-start(bf16[100,128,64]{0,2,1:T(8,128)(2,1)} %fusion.4), calls=%async_computation.1 | async-start | bytes 4194304 | tf_op jit(solution)/shard_map/all_to_all | solution.py:147
  193.4 7.4 %collective-permute-start.8 = (f32[7,32,64]{2,0,1:T(8,128)S(1)}, f32[7,32,64]{2,0,1:T(8,128)S(1)}, u32[]{:S(2)}, u32[]{:S(2)}) collective-permute-start(f32[7,32,64]{2,0,1:T(8,128)S(1)} %select_bitcast_fusion.2), channel_id=1, source_target_pairs={{0,1},{1,0},{2,3},{3,2},{4,5},{5,4},{6,7},{7,6},{8,9},{9,8},{10,11... | collective-permute-start | bytes 172040 | tf_op jit(solution)/shard_map/ppermute | solution.py:14
  279.9 20.2 %collective-permute-start.2 = (bf16[100,32,64]{0,2,1:T(8,128)(2,1)S(1)}, bf16[100,32,64]{0,2,1:T(8,128)(2,1)}, u32[]{:S(2)}, u32[]{:S(2)}) collective-permute-start(bf16[100,32,64]{0,2,1:T(8,128)(2,1)S(1)} %select_bitcast_fusion.1), channel_id=1, source_target_pairs={{0,1},{1,0},{2,3},{3,2},{4,5},{5,4},{6,7},{7,6},{8,9},{9,8},{10,11... | collective-permute-start | bytes 1228808 | tf_op jit(solution)/shard_map/ppermute | solution.py:14
  304.1 17.0 %all-to-all-start.2 = ((bf16[100,32,128]{2,0,1:T(8,128)(2,1)}), bf16[100,32,128]{2,0,1:T(8,128)(2,1)S(1)}, u32[]{:S(2)}, u32[]{:S(2)}) async-start(bf16[100,32,128]{2,0,1:T(8,128)(2,1)} %select_bitcast_fusion), calls=%async_computation.2 | async-start | bytes 1703936 | tf_op jit(solution)/shard_map/all_to_all | solution.py:176
where the time goes:
time: 323 us
  waiting for transfers between devices  120 us (37%)
  local copies, waits for them, and re-layouts  83.2 us (26%)
  starting transfers between devices  70.8 us (22%)
  other arithmetic  25.1 us (8%)
  blocking collectives  15.9 us (5%)
  matrix products  6.45 us (2%)
    all_to_all x1, waiting for transfers between devices, per_device(): lax.all_to_all(joined_coeffs, 'wide', split_axis=1, concat_axis=1, tiled=...  78.2 us
    gather x4, local copies, waits for them, and re-layouts, per_device(): gathered = jnp.take(extended, neighbours[face_index], axis=1)  56.8 us
    all_to_all x1, starting transfers between devices, per_device(): lax.all_to_all(pair_tags.astype(jnp.float32)[None, :], 'wide', split_axis...  17.8 us
    ppermute x5, waiting for transfers between devices, swapped(): lax.ppermute(value, axis, [(i, i ^ 1 << apart) for i in range(lax.axis_si...  17.6 us
    all_to_all x1, starting transfers between devices, per_device(): lax.all_to_all(joined_coeffs, 'wide', split_axis=1, concat_axis=1, tiled=...  16 us
    all_to_all x1, blocking collectives, per_device(): lax.all_to_all(relayed_stats, 'narrow', split_axis=1, concat_axis=1, tile...  15.9 us
    ppermute x4, starting transfers between devices, passed_along(): return lax.ppermute(value, axis, pairs)  14.8 us
    all_to_all x1, waiting for transfers between devices, per_device(): lax.all_to_all(relayed_coeffs, 'narrow', split_axis=1, concat_axis=1, til...  12.8 us
  transfers between devices with their start and end apart: 13, of which 6 were waited for; matrix products, arithmetic and copies ran while one was open for 11% of the time, Pallas kernels for 0%

commit v1 on v0

--- a/solution.py
+++ b/solution.py
@@ -174,7 +174,10 @@
     relayed_coeffs = jnp.take(whole_coeffs, through, axis=1)
     relayed_stats = jnp.take(whole_stats, through, axis=1)
     new_coeffs = lax.all_to_all(relayed_coeffs, "narrow", split_axis=1, concat_axis=1, tiled=True)
-    new_stats = lax.all_to_all(relayed_stats, "narrow", split_axis=1, concat_axis=1, tiled=True)
+    size = lax.axis_size("narrow")
+    shards = jnp.stack(jnp.split(relayed_stats, size, axis=1), axis=0)
+    shards = lax.all_to_all(shards, "narrow", split_axis=0, concat_axis=0)
+    new_stats = jnp.concatenate(shards, axis=1)
     flat_stats = new_stats.reshape(7, elem_count)
     return (new_coeffs.reshape(coeff_count, elem_count), flat_stats[:6], flat_stats[6])
 

time: 323 us -> 320 us (level)
  blocking collectives: 15.9 us -> 0 us
  waiting for transfers between devices: 120 us -> 127 us
  starting transfers between devices: 70.8 us -> 74.7 us
    all_to_all x1 -> x0, blocking collectives: 15.9 us -> none  [per_device(): lax.all_to_all(relayed_stats, 'narrow', split_axis=1, concat_axis=1, tile...]
    ppermute x5, waiting for transfers between devices: 17.6 us -> 26.6 us  [swapped(): lax.ppermute(value, axis, [(i, i ^ 1 << apart) for i in range(lax.axis_si...]
    all_to_all x0 -> x1, starting transfers between devices: none -> 3.99 us  [per_device(): shards = lax.all_to_all(shards, 'narrow', split_axis=0, concat_axis=0)]
  transfers between devices with their start and end apart: 13 -> 14, of which waited for: 6 -> 7; matrix products, arithmetic and copies ran while one was open for 11% -> 13% of each run, Pallas kernels for 0% -> 0%
where the time goes in v1:
time: 320 us; the launch traced here: 319 us
  waiting for transfers between devices  127 us (40%)
  local copies, waits for them, and re-layouts  83.9 us (26%)
  starting transfers between devices  74.7 us (23%)
  other arithmetic  25.1 us (8%)
  matrix products  6.45 us (2%)
    all_to_all x1, waiting for transfers between devices, per_device(): lax.all_to_all(joined_coeffs, 'wide', split_axis=1, concat_axis=1, tiled=...  77.5 us
    gather x4, local copies, waits for them, and re-layouts, per_device(): gathered = jnp.take(extended, neighbours[face_index], axis=1)  56.8 us
    ppermute x5, waiting for transfers between devices, swapped(): lax.ppermute(value, axis, [(i, i ^ 1 << apart) for i in range(lax.axis_si...  26.6 us
    all_to_all x1, starting transfers between devices, per_device(): lax.all_to_all(pair_tags.astype(jnp.float32)[None, :], 'wide', split_axis...  17.8 us
    all_to_all x1, starting transfers between devices, per_device(): lax.all_to_all(joined_coeffs, 'wide', split_axis=1, concat_axis=1, tiled=...  16 us
    ppermute x4, starting transfers between devices, passed_along(): return lax.ppermute(value, axis, pairs)  14.8 us
    ppermute x5, starting transfers between devices, swapped(): lax.ppermute(value, axis, [(i, i ^ 1 << apart) for i in range(lax.axis_si...  12.4 us
    all_to_all x1, waiting for transfers between devices, per_device(): lax.all_to_all(relayed_coeffs, 'narrow', split_axis=1, concat_axis=1, til...  12.3 us
  transfers between devices with their start and end apart: 14, of which 7 were waited for; matrix products, arithmetic and copies ran while one was open for 13% of the time, Pallas kernels for 0%

profile of v1, /device:TPU:32, one launch (start us, length us, event | category | flops | bytes accessed | tf_op | source)
XLA Modules:
  0.0 319.1 jit_solution(6815072162431226506)
XLA Ops:
  0.6 1.0 slice_reduce_fusion.3
  1.7 1.6 copy.56
  3.4 0.7 copy.59
  4.7 2.0 collective-permute-start.3
  7.4 5.7 %collective-permute-start.4 = (bf16[100,2,128]{2,0,1:T(8,128)(2,1)S(1)}, bf16[100,2,128]{2,0,1:T(8,128)(2,1)S(1)}, u32[]{:S(2)}, u32[]{:S(2)}) collective-permute-start(bf16[100,2,128]{2,0,1:T(8,128)(2,1)S(1)} %select_bitcast_fusion.6), channel_id=1, source_target_pairs={{0,508},{4,0},{8,4},{12,8},{16,12},{20,16},{24,20},{28,24},{32,28}... | collective-permute-start | bytes 153608 | tf_op jit(solution)/shard_map/ppermute | solution.py:10
  13.9 3.4 %collective-permute-start.5 = (bf16[100,2,128]{2,0,1:T(8,128)(2,1)S(1)}, bf16[100,2,128]{2,0,1:T(8,128)(2,1)S(1)}, u32[]{:S(2)}, u32[]{:S(2)}) collective-permute-start(bf16[100,2,128]{2,0,1:T(8,128)(2,1)S(1)} %select_bitcast_fusion.5), channel_id=1, source_target_pairs={{0,1},{1,2},{2,3},{3,0},{4,5},{5,6},{6,7},{7,4},{8,9},{9,10},{10,1... | collective-permute-start | bytes 153608 | tf_op jit(solution)/shard_map/ppermute | solution.py:10
  17.9 3.6 %collective-permute-start.6 = (bf16[100,2,128]{2,0,1:T(8,128)(2,1)S(1)}, bf16[100,2,128]{2,0,1:T(8,128)(2,1)S(1)}, u32[]{:S(2)}, u32[]{:S(2)}) collective-permute-start(bf16[100,2,128]{2,0,1:T(8,128)(2,1)S(1)} %select_bitcast_fusion.4), channel_id=1, source_target_pairs={{0,3},{1,0},{2,1},{3,2},{4,7},{5,4},{6,5},{7,6},{8,11},{9,8},{10,9... | collective-permute-start | bytes 153608 | tf_op jit(solution)/shard_map/ppermute | solution.py:10
  21.8 2.2 collective-permute-start
  24.9 1.4 fusion.28
  26.4 0.6 convert_element_type.36
  27.0 1.2 gather_fusion.3
  28.5 1.2 gather_fusion.4
  30.8 14.9 %gather_fusion.13 = bf16[4096,100]{1,0:T(8,128)(2,1)} fusion(bf16[100,5120]{0,1:T(8,128)(2,1)S(1)} %pad_maximum_fusion, s32[4096]{0:T(1024)S(1)} %fusion.38), kind=kCustom, calls=%fused_computation.4.clone | custom fusion | bytes 1654784 | tf_op jit(solution)/shard_map/jit(_take)/gather | solution.py:86
  45.7 14.9 %gather_fusion.14 = bf16[4096,100]{1,0:T(8,128)(2,1)} fusion(bf16[100,5120]{0,1:T(8,128)(2,1)S(1)} %pad_maximum_fusion, s32[4096]{0:T(1024)S(1)} %fusion.39), kind=kCustom, calls=%fused_computation.13.clone | custom fusion | bytes 1654784 | tf_op jit(solution)/shard_map/jit(_take)/gather | solution.py:86
  60.6 14.9 %gather_fusion.15 = bf16[4096,100]{1,0:T(8,128)(2,1)} fusion(bf16[100,5120]{0,1:T(8,128)(2,1)S(1)} %pad_maximum_fusion, s32[4096]{0:T(1024)S(1)} %fusion.40), kind=kCustom, calls=%fused_computation.14.clone | custom fusion | bytes 1654784 | tf_op jit(solution)/shard_map/jit(_take)/gather | solution.py:86
  75.4 12.1 %gather_fusion.16 = bf16[4096,100]{1,0:T(8,128)(2,1)S(1)} fusion(bf16[100,5120]{0,1:T(8,128)(2,1)S(1)} %pad_maximum_fusion, s32[4096]{0:T(1024)S(1)} %fusion.41), kind=kCustom, calls=%fused_computation.15.clone | custom fusion | bytes 1654784 | tf_op jit(solution)/shard_map/jit(_take)/gather | solution.py:86
  87.6 2.5 fusion.3
  90.1 0.8 fusion.2
  91.4 0.8 fusion.1
  92.2 0.8 fusion
  93.0 1.7 reshape.173
  94.8 4.4 %multiply_reduce_fusion = (f32[4096]{0:T(1024)S(1)}, f32[4096]{0:T(1024)S(1)}, f32[4096]{0:T(1024)S(1)}, f32[4096]{0:T(1024)S(1)}, f32[4096]{0:T(1024)S(1)}, /*index=5*/f32[4096]{0:T(1024)S(1)}) fusion(f32[25,3,4096]{2,1,0:T(4,128)} %reshape.173), kind=kLoop, calls=%fused_computation.56 | loop fusion | flops 1204224 | bytes 1327104 | tf_op jit(solution)/shard_map/reduce_sum | solution.py:30
  99.6 3.6 %collective-permute-start.7 = (f32[7,32,64]{2,0,1:T(8,128)S(1)}, f32[7,32,64]{2,0,1:T(8,128)S(1)}, u32[]{:S(2)}, u32[]{:S(2)}) collective-permute-start(f32[7,32,64]{2,0,1:T(8,128)S(1)} %get-tuple-element.43), channel_id=1, source_target_pairs={{0,1},{1,0},{2,3},{3,2},{4,5},{5,4},{6,7},{7,6},{8,9},{9,8},{10,11... | collective-permute-start | bytes 172040 | tf_op jit(solution)/shard_map/ppermute | solution.py:14
  103.3 0.7 copy.55
  104.0 17.8 %all-to-all-start = ((f32[1,128,1]{2,0,1:T(1,128)}), f32[1,128,1]{2,0,1:T(1,128)S(1)}, u32[]{:S(2)}, u32[]{:S(2)}) async-start(f32[1,128,1]{2,0,1:T(1,128)} %copy.55), calls=%async_computation | async-start | bytes 131072 | tf_op jit(solution)/shard_map/all_to_all | solution.py:143
  121.8 0.8 gather_fusion.17
  122.6 0.8 gather_fusion.18
  123.4 0.8 fusion.56
  124.2 1.1 reshape.406
  125.3 10.8 %all-to-all-done = f32[1,128,1]{2,0,1:T(1,128)S(1)} async-done(((f32[1,128,1]{2,0,1:T(1,128)}), f32[1,128,1]{2,0,1:T(1,128)S(1)}, u32[]{:S(2)}, u32[]{:S(2)}) %all-to-all-start) | async-done | bytes 544 | tf_op jit(solution)/shard_map/all_to_all | solution.py:143
  136.1 6.2 %all-to-all-start.3 = ((f32[128,1,448]{2,1,0:T(1,128)}), f32[128,1,448]{2,1,0:T(1,128)S(1)}, u32[]{:S(2)}, u32[]{:S(2)}) async-start(f32[128,1,448]{2,1,0:T(1,128)} %reshape.406), calls=%async_computation.3 | async-start | bytes 524288 | tf_op jit(solution)/shard_map/all_to_all | solution.py:142
  142.4 0.9 constant_dynamic-slice_fusion.1
  143.2 2.2 collective-permute-start.1
  145.4 1.0 gather_fusion.5
  146.4 12.9 %collective-permute-done.1 = bf16[100,32,64]{0,2,1:T(8,128)(2,1)S(1)} collective-permute-done((bf16[100,32,64]{0,2,1:T(8,128)(2,1)}, bf16[100,32,64]{0,2,1:T(8,128)(2,1)S(1)}, u32[]{:S(2)}, u32[]{:S(2)}) %collective-permute-start.1) | collective-permute-done | bytes 409632 | tf_op jit(solution)/shard_map/ppermute | solution.py:14
  159.3 2.2 gather_fusion.6
  161.5 3.3 %fusion.4 = bf16[100,128,64]{0,2,1:T(8,128)(2,1)} fusion(bf16[128,100,64]{1,2,0:T(8,128)(2,1)} %gather_fusion.6, bf16[128,100,64]{1,2,0:T(8,128)(2,1)S(1)} %gather_fusion.5, pred[128]{0:T(512)(128)(4,1)S(1)} %compare_and_fusion.9, pred[128]{0:T(512)(128)(4,1)S(1)} %copy-done.7, pred[128]{0:T(512)(128)(4,1)S(1)} %copy-done.6, pred[128]{0:T(512)(128)(4,1)S(1)} %fusion.36), kind=kLoop, calls=%fused_computation.30 | loop fusion | flops 3276800 | bytes 4915712 | tf_op jit(solution)/shard_map/jit(_where)/select_n | solution.py:124
  164.9 16.0 %all-to-all-start.1 = ((bf16[100,128,64]{0,2,1:T(8,128)(2,1)}), bf16[100,128,64]{0,2,1:T(8,128)(2,1)S(1)}, u32[]{:S(2)}, u32[]{:S(2)}) async-start(bf16[100,128,64]{0,2,1:T(8,128)(2,1)} %fusion.4), calls=%async_computation.1 | async-start | bytes 4194304 | tf_op jit(solution)/shard_map/all_to_all | solution.py:147
  180.9 2.4 convert_reduce_fusion
  183.3 2.5 sort.48
  185.9 0.7 gather_fusion
  186.6 2.5 sort.50
  189.1 1.6 sort.49
  191.3 1.3 reduce.16
  192.7 0.6 gather_fusion.20
  193.4 2.2 collective-permute-start.8
  195.6 0.6 gather_fusion.19
  196.2 4.6 %collective-permute-done.8 = f32[7,32,64]{2,0,1:T(8,128)S(1)} collective-permute-done((f32[7,32,64]{2,0,1:T(8,128)S(1)}, f32[7,32,64]{2,0,1:T(8,128)S(1)}, u32[]{:S(2)}, u32[]{:S(2)}) %collective-permute-start.8) | collective-permute-done | bytes 57376 | tf_op jit(solution)/shard_map/ppermute | solution.py:14
  201.7 77.5 %all-to-all-done.1 = bf16[100,128,64]{0,2,1:T(8,128)(2,1)S(1)} async-done(((bf16[100,128,64]{0,2,1:T(8,128)(2,1)}), bf16[100,128,64]{0,2,1:T(8,128)(2,1)S(1)}, u32[]{:S(2)}, u32[]{:S(2)}) %all-to-all-start.1) | async-done | bytes 1638432 | tf_op jit(solution)/shard_map/all_to_all | solution.py:147
  279.1 0.6 gather_fusion.8
  279.9 2.2 collective-permute-start.2
  282.3 0.7 copy.66
  282.9 4.0 %all-to-all-start.4 = ((f32[4,7,8,128]{3,2,1,0:T(8,128)}), f32[4,7,8,128]{3,2,1,0:T(8,128)S(1)}, u32[]{:S(2)}, u32[]{:S(2)}) async-start(f32[4,7,8,128]{3,2,1,0:T(8,128)} %copy.66), calls=%async_computation.4 | async-start | bytes 229376 | tf_op jit(solution)/shard_map/all_to_all | solution.py:179
  286.9 0.6 gather_fusion.7
  287.6 9.0 %collective-permute-done.2 = bf16[100,32,64]{0,2,1:T(8,128)(2,1)} collective-permute-done((bf16[100,32,64]{0,2,1:T(8,128)(2,1)S(1)}, bf16[100,32,64]{0,2,1:T(8,128)(2,1)}, u32[]{:S(2)}, u32[]{:S(2)}) %collective-permute-start.2) | collective-permute-done | bytes 409632 | tf_op jit(solution)/shard_map/ppermute | solution.py:14
  296.6 1.2 bitcast_select_fusion.3
  298.1 0.7 copy.57
  298.7 0.7 gather_fusion.1
  299.4 1.0 select_bitcast_fusion
  300.5 3.5 %all-to-all-start.2 = ((bf16[100,32,128]{2,0,1:T(8,128)(2,1)}), bf16[100,32,128]{2,0,1:T(8,128)(2,1)S(1)}, u32[]{:S(2)}, u32[]{:S(2)}) async-start(bf16[100,32,128]{2,0,1:T(8,128)(2,1)} %select_bitcast_fusion), calls=%async_computation.2 | async-start | bytes 1703936 | tf_op jit(solution)/shard_map/all_to_all | solution.py:176
  304.0 0.7 copy.74
  304.7 0.6 slice_bitcast_fusion.4
  305.4 12.3 %all-to-all-done.2 = bf16[100,32,128]{2,0,1:T(8,128)(2,1)S(1)} async-done(((bf16[100,32,128]{2,0,1:T(8,128)(2,1)}), bf16[100,32,128]{2,0,1:T(8,128)(2,1)S(1)}, u32[]{:S(2)}, u32[]{:S(2)}) %all-to-all-start.2) | async-done | bytes 819232 | tf_op jit(solution)/shard_map/all_to_all | solution.py:176
  317.9 1.2 copy.70
  (114 shorter events, 8.3 us)
Async XLA Ops:
  3.3 18.3 %copy-start.12 = (s32[32]{0:T(128)S(1)}, s32[32]{0:T(128)}, u32[]{:S(2)}) copy-start(s32[32]{0:T(128)} %param.24) | copy-start | bytes 388
  3.3 20.7 %copy-start.4 = (s32[4,4096]{1,0:T(4,128)S(1)}, s32[4,4096]{1,0:T(4,128)}, u32[]{:S(2)}) copy-start(s32[4,4096]{1,0:T(4,128)} %param.21) | copy-start | bytes 196612
  3.3 21.6 %copy-start.2 = (bf16[100,4096]{1,0:T(8,128)(2,1)S(1)}, bf16[100,4096]{1,0:T(8,128)(2,1)}, u32[]{:S(2)}) copy-start(bf16[100,4096]{1,0:T(8,128)(2,1)} %param.20) | copy-start | bytes 2457604
  3.3 21.6 %copy-start.3 = (bf16[5,75,100]{2,1,0:T(8,128)(2,1)S(1)}, bf16[5,75,100]{2,1,0:T(8,128)(2,1)}, u32[]{:S(2)}) copy-start(bf16[5,75,100]{2,1,0:T(8,128)(2,1)} %param.23) | copy-start | bytes 225004
  4.7 21.7 %copy-start.13 = (s32[32]{0:T(128)S(1)}, s32[32]{0:T(128)}, u32[]{:S(2)}) copy-start(s32[32]{0:T(128)} %param.25) | copy-start | bytes 388
  4.7 25.6 %collective-permute-start.3 = (bf16[100,2,128]{2,0,1:T(8,128)(2,1)S(1)}, bf16[100,2,128]{2,0,1:T(8,128)(2,1)S(1)}, u32[]{:S(2)}, u32[]{:S(2)}) collective-permute-start(bf16[100,2,128]{2,0,1:T(8,128)(2,1)S(1)} %select_bitcast_fusion.7), channel_id=1, source_target_pairs={{0,4},{4,8},{8,12},{12,16},{16,20},{20,24},{24,28},{28,32},{32,36}... | collective-permute-start | bytes 153608 | tf_op jit(solution)/shard_map/ppermute | solution.py:10
  7.4 22.8 %collective-permute-start.4 = (bf16[100,2,128]{2,0,1:T(8,128)(2,1)S(1)}, bf16[100,2,128]{2,0,1:T(8,128)(2,1)S(1)}, u32[]{:S(2)}, u32[]{:S(2)}) collective-permute-start(bf16[100,2,128]{2,0,1:T(8,128)(2,1)S(1)} %select_bitcast_fusion.6), channel_id=1, source_target_pairs={{0,508},{4,0},{8,4},{12,8},{16,12},{20,16},{24,20},{28,24},{32,28}... | collective-permute-start | bytes 153608 | tf_op jit(solution)/shard_map/ppermute | solution.py:10
  13.9 16.4 %collective-permute-start.5 = (bf16[100,2,128]{2,0,1:T(8,128)(2,1)S(1)}, bf16[100,2,128]{2,0,1:T(8,128)(2,1)S(1)}, u32[]{:S(2)}, u32[]{:S(2)}) collective-permute-start(bf16[100,2,128]{2,0,1:T(8,128)(2,1)S(1)} %select_bitcast_fusion.5), channel_id=1, source_target_pairs={{0,1},{1,2},{2,3},{3,0},{4,5},{5,6},{6,7},{7,4},{8,9},{9,10},{10,1... | collective-permute-start | bytes 153608 | tf_op jit(solution)/shard_map/ppermute | solution.py:10
  17.9 12.3 %collective-permute-start.6 = (bf16[100,2,128]{2,0,1:T(8,128)(2,1)S(1)}, bf16[100,2,128]{2,0,1:T(8,128)(2,1)S(1)}, u32[]{:S(2)}, u32[]{:S(2)}) collective-permute-start(bf16[100,2,128]{2,0,1:T(8,128)(2,1)S(1)} %select_bitcast_fusion.4), channel_id=1, source_target_pairs={{0,3},{1,0},{2,1},{3,2},{4,7},{5,4},{6,5},{7,6},{8,11},{9,8},{10,9... | collective-permute-start | bytes 153608 | tf_op jit(solution)/shard_map/ppermute | solution.py:10
  21.8 6.4 %collective-permute-start = (f32[2,32]{1,0:T(2,128)S(1)}, f32[2,32]{1,0:T(2,128)S(1)}, u32[]{:S(2)}, u32[]{:S(2)}) collective-permute-start(f32[2,32]{1,0:T(2,128)S(1)} %add_convert_fusion), channel_id=1, source_target_pairs={{0,1},{1,0},{2,3},{3,2},{4,5},{5,4},{6,7},{7,6},{8,9},{9,8},{10,11... | collective-permute-start | bytes 776 | tf_op jit(solution)/shard_map/ppermute | solution.py:14
  28.4 2.4 copy-start.10
  28.4 2.3 copy-start.5
  87.6 2.6 copy-start.1
  90.1 1.2 copy-start
  93.0 6.1 %copy-start.9 = (f32[32]{0:T(128)S(1)}, f32[32]{0:T(128)}, u32[]{:S(2)}) copy-start(f32[32]{0:T(128)} %convert_element_type.36) | copy-start | bytes 388
  94.7 8.5 %copy-start.11 = (s32[128]{0:T(128)S(1)}, s32[128]{0:T(128)}, u32[]{:S(2)}) copy-start(s32[128]{0:T(128)} %copy-done.10) | copy-start | bytes 1540
  94.8 8.5 %copy-start.8 = (f32[1,128,1]{1,2,0:T(1,128)S(1)}, f32[1,128,1]{1,2,0:T(1,128)}, u32[]{:S(2)}) copy-start(f32[1,128,1]{1,2,0:T(1,128)} %convert_bitcast_fusion) | copy-start | bytes 1540
  99.1 24.2 %copy-start.6 = (pred[128]{0:T(512)(128)(4,1)S(1)}, pred[128]{0:T(512)(128)(4,1)}, u32[]{:S(2)}) copy-start(pred[128]{0:T(512)(128)(4,1)} %copy-done.5) | copy-start | bytes 388
  99.1 24.2 %copy-start.7 = (pred[128]{0:T(512)(128)(4,1)S(1)}, pred[128]{0:T(512)(128)(4,1)}, u32[]{:S(2)}) copy-start(pred[128]{0:T(512)(128)(4,1)} %compare_and_fusion.10) | copy-start | bytes 388
  99.6 23.0 %collective-permute-start.7 = (f32[7,32,64]{2,0,1:T(8,128)S(1)}, f32[7,32,64]{2,0,1:T(8,128)S(1)}, u32[]{:S(2)}, u32[]{:S(2)}) collective-permute-start(f32[7,32,64]{2,0,1:T(8,128)S(1)} %get-tuple-element.43), channel_id=1, source_target_pairs={{0,1},{1,0},{2,3},{3,2},{4,5},{5,4},{6,7},{7,6},{8,9},{9,8},{10,11... | collective-permute-start | bytes 172040 | tf_op jit(solution)/shard_map/ppermute | solution.py:14
  104.0 32.1 %all-to-all-start = ((f32[1,128,1]{2,0,1:T(1,128)}), f32[1,128,1]{2,0,1:T(1,128)S(1)}, u32[]{:S(2)}, u32[]{:S(2)}) async-start(f32[1,128,1]{2,0,1:T(1,128)} %copy.55), calls=%async_computation | async-start | bytes 131072 | tf_op jit(solution)/shard_map/all_to_all | solution.py:143
  136.1 28.8 %all-to-all-start.3 = ((f32[128,1,448]{2,1,0:T(1,128)}), f32[128,1,448]{2,1,0:T(1,128)S(1)}, u32[]{:S(2)}, u32[]{:S(2)}) async-start(f32[128,1,448]{2,1,0:T(1,128)} %reshape.406), calls=%async_computation.3 | async-start | bytes 524288 | tf_op jit(solution)/shard_map/all_to_all | solution.py:142
  143.2 16.1 %collective-permute-start.1 = (bf16[100,32,64]{0,2,1:T(8,128)(2,1)}, bf16[100,32,64]{0,2,1:T(8,128)(2,1)S(1)}, u32[]{:S(2)}, u32[]{:S(2)}) collective-permute-start(bf16[100,32,64]{0,2,1:T(8,128)(2,1)} %get-tuple-element.39), channel_id=1, source_target_pairs={{0,1},{1,0},{2,3},{3,2},{4,5},{5,4},{6,7},{7,6},{8,9},{9,8},{10,11... | collective-permute-start | bytes 1228808 | tf_op jit(solution)/shard_map/ppermute | solution.py:14
  164.9 114.2 %all-to-all-start.1 = ((bf16[100,128,64]{0,2,1:T(8,128)(2,1)}), bf16[100,128,64]{0,2,1:T(8,128)(2,1)S(1)}, u32[]{:S(2)}, u32[]{:S(2)}) async-start(bf16[100,128,64]{0,2,1:T(8,128)(2,1)} %fusion.4), calls=%async_computation.1 | async-start | bytes 4194304 | tf_op jit(solution)/shard_map/all_to_all | solution.py:147
  193.4 7.4 %collective-permute-start.8 = (f32[7,32,64]{2,0,1:T(8,128)S(1)}, f32[7,32,64]{2,0,1:T(8,128)S(1)}, u32[]{:S(2)}, u32[]{:S(2)}) collective-permute-start(f32[7,32,64]{2,0,1:T(8,128)S(1)} %select_bitcast_fusion.2), channel_id=1, source_target_pairs={{0,1},{1,0},{2,3},{3,2},{4,5},{5,4},{6,7},{7,6},{8,9},{9,8},{10,11... | collective-permute-start | bytes 172040 | tf_op jit(solution)/shard_map/ppermute | solution.py:14
  279.9 16.7 %collective-permute-start.2 = (bf16[100,32,64]{0,2,1:T(8,128)(2,1)S(1)}, bf16[100,32,64]{0,2,1:T(8,128)(2,1)}, u32[]{:S(2)}, u32[]{:S(2)}) collective-permute-start(bf16[100,32,64]{0,2,1:T(8,128)(2,1)S(1)} %select_bitcast_fusion.1), channel_id=1, source_target_pairs={{0,1},{1,0},{2,3},{3,2},{4,5},{5,4},{6,7},{7,6},{8,9},{9,8},{10,11... | collective-permute-start | bytes 1228808 | tf_op jit(solution)/shard_map/ppermute | solution.py:14
  282.9 17.6 %all-to-all-start.4 = ((f32[4,7,8,128]{3,2,1,0:T(8,128)}), f32[4,7,8,128]{3,2,1,0:T(8,128)S(1)}, u32[]{:S(2)}, u32[]{:S(2)}) async-start(f32[4,7,8,128]{3,2,1,0:T(8,128)} %copy.66), calls=%async_computation.4 | async-start | bytes 229376 | tf_op jit(solution)/shard_map/all_to_all | solution.py:179
  300.5 17.2 %all-to-all-start.2 = ((bf16[100,32,128]{2,0,1:T(8,128)(2,1)}), bf16[100,32,128]{2,0,1:T(8,128)(2,1)S(1)}, u32[]{:S(2)}, u32[]{:S(2)}) async-start(bf16[100,32,128]{2,0,1:T(8,128)(2,1)} %select_bitcast_fusion), calls=%async_computation.2 | async-start | bytes 1703936 | tf_op jit(solution)/shard_map/all_to_all | solution.py:176
